TPU v7x, 32 devices: a whole 2x2x4 slice. The times are simulated.
32 devices in a mesh: row: 4 (over y, x), col: 8 (over z, core).
Axes of the slice: x: 2, y: 2, z: 4, core: 2. Of those that a mesh axis runs over, the one named last changes fastest.
Arguments:
- galaxy: float32 [128, 256, 256], P('row', 'col'), may hold values from 0.03 to 32, as said below
- randoms: float32 [128, 256, 256], P('row', 'col'), may hold values from 0.5 to 4
- coverage: int32 [128, 256, 256], P('row', 'col'), may hold values from 0 to 1
- patch: int32 [128, 256, 256], P('row', 'col'), may hold values from 0 to 127
Outputs:
- contrast: float32 [128, 256, 256], P('row', 'col')
- patch_sums: float32 [4, 128], replicated
Inputs may be any that keep to these rules, and one draw needn't show every extreme that they name: `galaxy`: positive densities.
All inputs are finite; a program needn't handle non-finite values.
Results may differ from a plain program's by a relative error of at most 0.00016.
Values sent between devices are 32-bit elements; how exact they have to be, the bound alone decides.
A program may use at most 64 MiB of HBM per device.

v0:
```python
import jax
import jax.numpy as jnp
from jax import lax
from jax.sharding import PartitionSpec as P

RADIUS = 16
NPATCH = 128


def extended_2(array, sides, width):
    for axis, dim in sides:
        devices, length = (lax.axis_size(axis), array.shape[dim])
        up = [(i, (i + 1) % devices) for i in range(devices - 1)]
        down = [(j, i) for i, j in up]
        last = lax.slice_in_dim(array, length - width, length, axis=dim)
        first = lax.slice_in_dim(array, 0, width, axis=dim)
        before = lax.ppermute(last, axis, up)
        after = lax.ppermute(first, axis, down)
        array = jnp.concatenate([before, array, after], axis=dim)
    return array


def kernel_taps(radius):
    offs = jnp.arange(-radius, radius + 1).astype(jnp.float32)
    sigma = radius / 2.0
    vals = jnp.exp(-offs * offs / (2.0 * sigma * sigma))
    return vals / jnp.sum(vals)


def valid_taps(padded, taps, radius, axis):
    count = padded.shape[axis] - 2 * radius
    total = lax.slice_in_dim(padded, 0, count, axis=axis) * taps[0]
    for j in range(1, 2 * radius + 1):
        total = total + taps[j] * lax.slice_in_dim(padded, j, j + count, axis=axis)
    return total


def local(galaxy, randoms, coverage, patch):
    radius = RADIUS
    taps = kernel_taps(radius)
    fields = jnp.stack([galaxy, randoms])
    widths = ((0, 0), (0, 0), (0, 0), (radius, radius))
    zsmooth = valid_taps(jnp.pad(fields, widths), taps, radius, 3)
    cover = coverage.astype(jnp.float32)
    totals = lax.psum((jnp.sum(cover * galaxy), jnp.sum(cover * randoms)), ("row", "col"))
    extended = extended_2(zsmooth, (("row", 1), ("col", 2)), radius)
    xsmooth = valid_taps(extended, taps, radius, 1)
    smoothed = valid_taps(xsmooth, taps, radius, 2)
    alpha = totals[0] / totals[1]
    nbar = alpha * smoothed[1]
    weight = 1.0 / (1.0 + 2.0 * nbar)
    contrast = cover * weight * (smoothed[0] / nbar - 1.0)
    rows_x, rows_y, depth = contrast.shape
    per_row = rows_y * depth
    block = 1
    for cand in range(1, rows_x + 1):
        if rows_x % cand == 0 and cand * per_row <= 32768:
            block = cand
    steps_count = rows_x // block
    flat_c = contrast.reshape(steps_count, block * per_row)
    flat_m = cover.reshape(steps_count, block * per_row)
    flat_p = patch.reshape(steps_count, block * per_row)
    labels = jnp.arange(NPATCH, dtype=jnp.int32)

    def accumulate(carry, items):
        cvals, mvals, pvals = items
        powers = jnp.stack(
            [mvals, mvals * cvals, mvals * cvals * cvals, mvals * cvals * cvals * cvals]
        )
        onehot = (pvals[None, :] == labels[:, None]).astype(jnp.float32)
        part_sums = lax.dot_general(
            powers,
            onehot,
            (((1,), (1,)), ((), ())),
            precision=lax.Precision.HIGHEST,
            preferred_element_type=jnp.float32,
        )
        return (carry + part_sums, None)

    local_sums, unused = lax.scan(
        accumulate, jnp.zeros((4, NPATCH), jnp.float32), (flat_c, flat_m, flat_p)
    )
    whole_sums = lax.psum(local_sums, ("row", "col"))
    scale = NPATCH / (rows_x * lax.axis_size("row") * rows_y * lax.axis_size("col") * depth)
    return (contrast, whole_sums * scale)


def solution(mesh):
    in_specs = (
        P("row", "col", None),
        P("row", "col", None),
        P("row", "col", None),
        P("row", "col", None),
    )
    out_specs = (P("row", "col", None), P())
    return jax.shard_map(local, mesh=mesh, in_specs=in_specs, out_specs=out_specs, check_vma=False)
```

profile of v0, /device:TPU:0, one launch (start us, length us, event | category | flops | bytes accessed | tf_op | source)
XLA Modules:
  0.0 384.6 jit_solution(8935265958357768094)
XLA Ops:
  3.4 3.1 pad_maximum_fusion.2
  6.5 64.2 %fusion.99 = f32[2,32,32,256]{3,2,1,0:T(8,128)S(1)} fusion(f32[2,32,32,256]{3,2,1,0:T(8,128)} %pad_maximum_fusion.2, f32[]{:T(128)} %bitcast.34, f32[]{:T(128)} %bitcast.33, f32[]{:T(128)} %bitcast.32, f32[]{:T(128)} %bitcast.31, f32[]{:T(128)} %bitcast.30, f32[]{:T(128)} %bitcast.29, f32[]{:T(128)} %bitcast.28, f32[]{:T(128)} %bitcast.27, f32[]{:T(128)} %bitcast.26, ...), kind=kLoop, calls=%fused_computation.171 | loop fusion | flops 34078720 | bytes 4194436 | tf_op jit(solution)/shard_map/add | solution.py:34
  70.9 4.9 %collective-permute-start = (f32[2,16,32,256]{3,2,1,0:T(8,128)S(1)}, f32[2,16,32,256]{3,2,1,0:T(8,128)S(1)}, u32[]{:S(2)}, u32[]{:S(2)}) collective-permute-start(f32[2,16,32,256]{3,2,1,0:T(8,128)S(1)} %get-tuple-element.75), channel_id=1, source_target_pairs={{0,8},{8,16},{16,24},{1,9},{9,17},{17,25},{2,10},{10,18},{18,26},{... | collective-permute-start | bytes 3145736 | tf_op jit(solution)/shard_map/ppermute | solution.py:17
  77.2 21.0 %collective-permute-done = f32[2,16,32,256]{3,2,1,0:T(8,128)S(1)} collective-permute-done((f32[2,16,32,256]{3,2,1,0:T(8,128)S(1)}, f32[2,16,32,256]{3,2,1,0:T(8,128)S(1)}, u32[]{:S(2)}, u32[]{:S(2)}) %collective-permute-start) | collective-permute-done | bytes 1048608 | tf_op jit(solution)/shard_map/ppermute | solution.py:17
  98.2 24.4 %collective-permute-done.1 = f32[2,16,32,256]{3,2,1,0:T(8,128)S(1)} collective-permute-done((f32[2,16,32,256]{3,2,1,0:T(8,128)S(1)}, f32[2,16,32,256]{3,2,1,0:T(8,128)S(1)}, u32[]{:S(2)}, u32[]{:S(2)}) %collective-permute-start.1) | collective-permute-done | bytes 1048608 | tf_op jit(solution)/shard_map/ppermute | solution.py:18
  123.7 2.4 fusion.147
  126.1 2.6 collective-permute-start.2
  131.1 46.6 %all-reduce.1 = (f32[]{:T(128)}, f32[]{:T(128)}) all-reduce(f32[]{:T(128)} %get-tuple-element.56, f32[]{:T(128)} %get-tuple-element.55), channel_id=1, replica_groups=mesh['row'=4,'col'=8] {'row','col'}, use_global_device_ids=true, to_apply=%region_1.2 | all-reduce | flops 2 | bytes 16 | tf_op jit(solution)/shard_map/psum | solution.py:45
  178.8 2.5 reshape.25
  181.3 2.4 reshape.27
  185.0 3.3 pad_maximum_fusion
  188.3 36.4 %fusion.13 = f32[2,32,64,256]{3,2,1,0:T(8,128)S(1)} fusion(f32[2,64,64,256]{3,2,1,0:T(8,128)S(1)} %pad_maximum_fusion, f32[]{:T(128)} %bitcast.34, f32[]{:T(128)} %bitcast.33, f32[]{:T(128)} %bitcast.32, f32[]{:T(128)} %bitcast.31, f32[]{:T(128)} %bitcast.30, f32[]{:T(128)} %bitcast.29, f32[]{:T(128)} %bitcast.28, f32[]{:T(128)} %bitcast.27, f32[]{:T(128)} %bitcast.26, ...), kind=kLoop, calls=%fused_computation.52 | loop fusion | flops 68157440 | bytes 142606464 | tf_op jit(solution)/shard_map/add | solution.py:34
  224.8 28.9 %fusion.109 = f32[2,32,32,256]{3,2,1,0:T(8,128)S(1)} fusion(f32[2,32,64,256]{3,2,1,0:T(8,128)S(1)} %fusion.13, f32[]{:T(128)} %bitcast.34, f32[]{:T(128)} %bitcast.33, f32[]{:T(128)} %bitcast.32, f32[]{:T(128)} %bitcast.31, f32[]{:T(128)} %bitcast.30, f32[]{:T(128)} %bitcast.29, f32[]{:T(128)} %bitcast.28, f32[]{:T(128)} %bitcast.27, f32[]{:T(128)} %bitcast.26, ...), kind=kLoop, calls=%fused_computation.182 | loop fusion | flops 34078720 | bytes 71303296 | tf_op jit(solution)/shard_map/add | solution.py:34
  255.0 87.6 %while.11 = (s32[]{:T(128)}, f32[4,128]{1,0:T(4,128)S(1)}, f32[8,32768]{1,0:T(8,128)}, f32[8,32768]{1,0:T(8,128)S(1)}, s32[8,32768]{1,0:T(8,128)}, /*index=5*/s32[]{:T(128)}, s32[]{:T(128)}) while((s32[]{:T(128)}, f32[4,128]{1,0:T(4,128)S(1)}, f32[8,32768]{1,0:T(8,128)}, f32[8,32768]{1,0:T(8,128)S(1)}, s32[8,32768]{1,0:T(8,128)}, ...), condition=%wide.region_6.7_spmd.clone, body=%wide.region_5.6_spmd.clone.sunk | while | flops 206013440 | bytes 1708127 | solution.py:80
  255.0 1.5 dynamic-slice_multiply_fusion.6
  257.8 8.1 %fusion.154 = f32[4,128]{1,0:T(4,128)S(1)} fusion(s32[32768]{0:T(1024)S(1)} %bitcast.48, f32[1,32768]{1,0:T(1,128)S(1)} %get-tuple-element.145, f32[1,32768]{1,0:T(1,128)S(1)} %get-tuple-element.146, f32[1,32768]{1,0:T(1,128)S(1)} %get-tuple-element.147, f32[1,32768]{1,0:T(1,128)S(1)} %get-tuple-element.148, f32[4,128]{1,0:T(4,128)S(1)} %get-tuple-element.157, ...), kind=kOutput, calls=%fused_computation.4.clone.1 | convolution fusion | flops 205915136 | bytes 659457 | tf_op jit(solution)/shard_map/while/body/eval_jaxpr/dot_general | solution.py:71
  265.9 1.5 dynamic-slice_multiply_fusion.6
  268.8 8.1 %fusion.154 = f32[4,128]{1,0:T(4,128)S(1)} fusion(s32[32768]{0:T(1024)S(1)} %bitcast.48, f32[1,32768]{1,0:T(1,128)S(1)} %get-tuple-element.145, f32[1,32768]{1,0:T(1,128)S(1)} %get-tuple-element.146, f32[1,32768]{1,0:T(1,128)S(1)} %get-tuple-element.147, f32[1,32768]{1,0:T(1,128)S(1)} %get-tuple-element.148, f32[4,128]{1,0:T(4,128)S(1)} %get-tuple-element.157, ...), kind=kOutput, calls=%fused_computation.4.clone.1 | convolution fusion | flops 205915136 | bytes 659457 | tf_op jit(solution)/shard_map/while/body/eval_jaxpr/dot_general | solution.py:71
  276.9 1.5 dynamic-slice_multiply_fusion.6
  278.4 1.3 constant_dynamic-slice_fusion.3
  279.7 8.1 %fusion.154 = f32[4,128]{1,0:T(4,128)S(1)} fusion(s32[32768]{0:T(1024)S(1)} %bitcast.48, f32[1,32768]{1,0:T(1,128)S(1)} %get-tuple-element.145, f32[1,32768]{1,0:T(1,128)S(1)} %get-tuple-element.146, f32[1,32768]{1,0:T(1,128)S(1)} %get-tuple-element.147, f32[1,32768]{1,0:T(1,128)S(1)} %get-tuple-element.148, f32[4,128]{1,0:T(4,128)S(1)} %get-tuple-element.157, ...), kind=kOutput, calls=%fused_computation.4.clone.1 | convolution fusion | flops 205915136 | bytes 659457 | tf_op jit(solution)/shard_map/while/body/eval_jaxpr/dot_general | solution.py:71
  287.9 1.5 dynamic-slice_multiply_fusion.6
  290.7 8.1 %fusion.154 = f32[4,128]{1,0:T(4,128)S(1)} fusion(s32[32768]{0:T(1024)S(1)} %bitcast.48, f32[1,32768]{1,0:T(1,128)S(1)} %get-tuple-element.145, f32[1,32768]{1,0:T(1,128)S(1)} %get-tuple-element.146, f32[1,32768]{1,0:T(1,128)S(1)} %get-tuple-element.147, f32[1,32768]{1,0:T(1,128)S(1)} %get-tuple-element.148, f32[4,128]{1,0:T(4,128)S(1)} %get-tuple-element.157, ...), kind=kOutput, calls=%fused_computation.4.clone.1 | convolution fusion | flops 205915136 | bytes 659457 | tf_op jit(solution)/shard_map/while/body/eval_jaxpr/dot_general | solution.py:71
  298.8 1.5 dynamic-slice_multiply_fusion.6
  301.7 8.1 %fusion.154 = f32[4,128]{1,0:T(4,128)S(1)} fusion(s32[32768]{0:T(1024)S(1)} %bitcast.48, f32[1,32768]{1,0:T(1,128)S(1)} %get-tuple-element.145, f32[1,32768]{1,0:T(1,128)S(1)} %get-tuple-element.146, f32[1,32768]{1,0:T(1,128)S(1)} %get-tuple-element.147, f32[1,32768]{1,0:T(1,128)S(1)} %get-tuple-element.148, f32[4,128]{1,0:T(4,128)S(1)} %get-tuple-element.157, ...), kind=kOutput, calls=%fused_computation.4.clone.1 | convolution fusion | flops 205915136 | bytes 659457 | tf_op jit(solution)/shard_map/while/body/eval_jaxpr/dot_general | solution.py:71
  309.8 1.5 dynamic-slice_multiply_fusion.6
  312.6 8.1 %fusion.154 = f32[4,128]{1,0:T(4,128)S(1)} fusion(s32[32768]{0:T(1024)S(1)} %bitcast.48, f32[1,32768]{1,0:T(1,128)S(1)} %get-tuple-element.145, f32[1,32768]{1,0:T(1,128)S(1)} %get-tuple-element.146, f32[1,32768]{1,0:T(1,128)S(1)} %get-tuple-element.147, f32[1,32768]{1,0:T(1,128)S(1)} %get-tuple-element.148, f32[4,128]{1,0:T(4,128)S(1)} %get-tuple-element.157, ...), kind=kOutput, calls=%fused_computation.4.clone.1 | convolution fusion | flops 205915136 | bytes 659457 | tf_op jit(solution)/shard_map/while/body/eval_jaxpr/dot_general | solution.py:71
  320.7 1.5 dynamic-slice_multiply_fusion.6
  323.6 8.1 %fusion.154 = f32[4,128]{1,0:T(4,128)S(1)} fusion(s32[32768]{0:T(1024)S(1)} %bitcast.48, f32[1,32768]{1,0:T(1,128)S(1)} %get-tuple-element.145, f32[1,32768]{1,0:T(1,128)S(1)} %get-tuple-element.146, f32[1,32768]{1,0:T(1,128)S(1)} %get-tuple-element.147, f32[1,32768]{1,0:T(1,128)S(1)} %get-tuple-element.148, f32[4,128]{1,0:T(4,128)S(1)} %get-tuple-element.157, ...), kind=kOutput, calls=%fused_computation.4.clone.1 | convolution fusion | flops 205915136 | bytes 659457 | tf_op jit(solution)/shard_map/while/body/eval_jaxpr/dot_general | solution.py:71
  331.7 1.5 dynamic-slice_multiply_fusion.6
  334.5 8.1 %fusion.154 = f32[4,128]{1,0:T(4,128)S(1)} fusion(s32[32768]{0:T(1024)S(1)} %bitcast.48, f32[1,32768]{1,0:T(1,128)S(1)} %get-tuple-element.145, f32[1,32768]{1,0:T(1,128)S(1)} %get-tuple-element.146, f32[1,32768]{1,0:T(1,128)S(1)} %get-tuple-element.147, f32[1,32768]{1,0:T(1,128)S(1)} %get-tuple-element.148, f32[4,128]{1,0:T(4,128)S(1)} %get-tuple-element.157, ...), kind=kOutput, calls=%fused_computation.4.clone.1 | convolution fusion | flops 205915136 | bytes 659457 | tf_op jit(solution)/shard_map/while/body/eval_jaxpr/dot_general | solution.py:71
  342.6 41.4 %psum.23 = f32[4,128]{1,0:T(4,128)S(1)} all-reduce(f32[4,128]{1,0:T(4,128)S(1)} %get-tuple-element.34), channel_id=1, replica_groups=mesh['row'=4,'col'=8] {'row','col'}, use_global_device_ids=true, to_apply=%region_7.8 | all-reduce | flops 512 | bytes 4096 | tf_op jit(solution)/shard_map/psum | solution.py:83
  (35 shorter events, 19.9 us)
Async XLA Ops:
  70.9 27.2 %collective-permute-start = (f32[2,16,32,256]{3,2,1,0:T(8,128)S(1)}, f32[2,16,32,256]{3,2,1,0:T(8,128)S(1)}, u32[]{:S(2)}, u32[]{:S(2)}) collective-permute-start(f32[2,16,32,256]{3,2,1,0:T(8,128)S(1)} %get-tuple-element.75), channel_id=1, source_target_pairs={{0,8},{8,16},{16,24},{1,9},{9,17},{17,25},{2,10},{10,18},{18,26},{... | collective-permute-start | bytes 3145736 | tf_op jit(solution)/shard_map/ppermute | solution.py:17
  75.9 46.8 %collective-permute-start.1 = (f32[2,16,32,256]{3,2,1,0:T(8,128)S(1)}, f32[2,16,32,256]{3,2,1,0:T(8,128)S(1)}, u32[]{:S(2)}, u32[]{:S(2)}) collective-permute-start(f32[2,16,32,256]{3,2,1,0:T(8,128)S(1)} %get-tuple-element.76), channel_id=1, source_target_pairs={{8,0},{16,8},{24,16},{9,1},{17,9},{25,17},{10,2},{18,10},{26,18},{... | collective-permute-start | bytes 3145736 | tf_op jit(solution)/shard_map/ppermute | solution.py:18
  98.2 25.1 %copy-start.4 = (f32[2,16,32,256]{3,2,1,0:T(8,128)}, f32[2,16,32,256]{3,2,1,0:T(8,128)S(1)}, u32[]{:S(2)}) copy-start(f32[2,16,32,256]{3,2,1,0:T(8,128)S(1)} %collective-permute-done) | copy-start | bytes 3145732
  122.6 1.1 copy-start.5
  123.7 6.3 %copy-start = (s32[32,32,256]{2,1,0:T(8,128)S(1)}, s32[32,32,256]{2,1,0:T(8,128)}, u32[]{:S(2)}) copy-start(s32[32,32,256]{2,1,0:T(8,128)} %param.8) | copy-start | bytes 3145732
  123.7 6.3 %copy-start.2 = (f32[32,32,256]{2,1,0:T(8,128)S(1)}, f32[32,32,256]{2,1,0:T(8,128)}, u32[]{:S(2)}) copy-start(f32[32,32,256]{2,1,0:T(8,128)} %param.7) | copy-start | bytes 3145732
  123.7 6.3 %copy-start.3 = (f32[32,32,256]{2,1,0:T(8,128)S(1)}, f32[32,32,256]{2,1,0:T(8,128)}, u32[]{:S(2)}) copy-start(f32[32,32,256]{2,1,0:T(8,128)} %param.6) | copy-start | bytes 3145732
  126.1 58.9 %collective-permute-start.2 = (f32[2,64,16,256]{3,2,1,0:T(8,128)}, f32[2,64,16,256]{3,2,1,0:T(8,128)}, u32[]{:S(2)}, u32[]{:S(2)}) collective-permute-start(f32[2,64,16,256]{3,2,1,0:T(8,128)} %get-tuple-element.73), channel_id=1, source_target_pairs={{0,1},{1,2},{2,3},{3,4},{4,5},{5,6},{6,7},{8,9},{9,10},{10,11},{11... | collective-permute-start | bytes 6291464 | tf_op jit(solution)/shard_map/ppermute | solution.py:17
  128.7 56.3 %collective-permute-start.3 = (f32[2,64,16,256]{3,2,1,0:T(8,128)}, f32[2,64,16,256]{3,2,1,0:T(8,128)}, u32[]{:S(2)}, u32[]{:S(2)}) collective-permute-start(f32[2,64,16,256]{3,2,1,0:T(8,128)} %get-tuple-element.74), channel_id=1, source_target_pairs={{1,0},{2,1},{3,2},{4,3},{5,4},{6,5},{7,6},{9,8},{10,9},{11,10},{12... | collective-permute-start | bytes 6291464 | tf_op jit(solution)/shard_map/ppermute | solution.py:18
  254.0 1.0 copy-start.1
where the time goes:
time: 387 us; the launch traced here: 385 us
  other arithmetic  153 us (40%)
  blocking collectives  88 us (23%)
  matrix products  64.8 us (17%)
  waiting for transfers between devices  45.5 us (12%)
  local copies, waits for them, and re-layouts  20.9 us (5%)
  starting transfers between devices  10.1 us (3%)
    add x3, other arithmetic, valid_taps(): total = total + taps[j] * lax.slice_in_dim(padded, j, j + count, axis=axis)  130 us
    dot_general x8, matrix products, accumulate(): lax.dot_general(powers, onehot, (((1,), (1,)), ((), ())), precision=lax.P...  64.8 us
    psum x1, blocking collectives, local(): lax.psum((jnp.sum(cover * galaxy), jnp.sum(cover * randoms)), ('row', 'co...  46.6 us
    psum x1, blocking collectives, local(): whole_sums = lax.psum(local_sums, ('row', 'col'))  41.4 us
    ppermute x2, waiting for transfers between devices, extended_2(): after = lax.ppermute(first, axis, down)  24.4 us
    ppermute x2, waiting for transfers between devices, extended_2(): before = lax.ppermute(last, axis, up)  21 us
    mul x8, other arithmetic, accumulate(): mvals * cvals * cvals * cvals  12 us
    dynamic_slice x8, local copies, waits for them, and re-layouts, local(): lax.scan(accumulate, jnp.zeros((4, NPATCH), jnp.float32), (flat_c, flat_m...  10.6 us
  transfers between devices with their start and end apart: 4, of which 2 were waited for; matrix products, arithmetic and copies ran while one was open for 2% of the time, Pallas kernels for 0%

commit v1 on v0

v1 whole, which is shorter than its diff:
```python
import functools

import jax
import jax.numpy as jnp
import ml_dtypes
import numpy as np
from jax import lax
from jax.experimental import pallas as pl
from jax.experimental.pallas import tpu as pltpu
from jax.sharding import PartitionSpec as P

RADIUS = 16
NPATCH = 128
LANES = 128
F32 = jnp.float32
BF16 = jnp.bfloat16
MESH = pl.DeviceIdType.MESH


def taps_np():
    offs = np.arange(-RADIUS, RADIUS + 1).astype(np.float32)
    sigma = RADIUS / 2.0
    vals = np.exp(-offs * offs / np.float32(2.0 * sigma * sigma)).astype(np.float32)
    return (vals / vals.sum(dtype=np.float32)).astype(np.float32)


def split_np(mat):
    high = mat.astype(ml_dtypes.bfloat16)
    low = (mat - high.astype(np.float32)).astype(ml_dtypes.bfloat16)
    return high, low


def band(outs, ins, shift):
    taps = taps_np()
    mat = np.zeros((outs, ins), np.float32)
    for o in range(outs):
        for j in range(-RADIUS, RADIUS + 1):
            i = o + j + shift
            if 0 <= i < ins:
                mat[o, i] = taps[j + RADIUS]
    return mat


def split(val):
    high = val.astype(BF16)
    low = (val - high.astype(F32)).astype(BF16)
    return high, low


def dot(a, b):
    return jnp.dot(a, b, preferred_element_type=F32)


def gather_sum(axis, size, buf, send, recv):
    me = lax.axis_index(axis)
    copies = []
    for k in range(1, size):
        copy = pltpu.make_async_remote_copy(
            src_ref=buf.at[me],
            dst_ref=buf.at[me],
            send_sem=send.at[k - 1],
            recv_sem=recv.at[k - 1],
            device_id={axis: lax.rem(me + k, size)},
            device_id_type=MESH,
        )
        copy.start()
        copies.append(copy)
    return copies


def add_up(copies, buf, size):
    for copy in copies:
        copy.wait()
    total = buf[0]
    for k in range(1, size):
        total = total + buf[k]
    return total


def kernel(
    rows, cols, scale,
    gal, ran, cov, pat, thi, tlo, kxhi, kxlo, kyhi, kylo, rep,
    contrast, sums,
    xb, yb, acc, trow, tcol, srow, scol,
    sx, rx, sy, ry, s1, r1, s2, r2, s3, r3, s4, r4,
):
    X, Y, Z = gal.shape
    halves = Z // LANES
    W = RADIUS
    me_r = lax.axis_index("row")
    me_c = lax.axis_index("col")

    barrier = pltpu.get_barrier_semaphore()
    for k in range(1, rows):
        pl.semaphore_signal(barrier, inc=1, device_id={"row": lax.rem(me_r + k, rows)}, device_id_type=MESH)
    for k in range(1, cols):
        pl.semaphore_signal(barrier, inc=1, device_id={"col": lax.rem(me_c + k, cols)}, device_id_type=MESH)
    pl.semaphore_wait(barrier, rows + cols - 2)

    def xcopy(h, up):
        own, far = ((X, 0) if up else (W, X + W))
        return pltpu.make_async_remote_copy(
            src_ref=xb.at[h, :, pl.ds(own, W)],
            dst_ref=xb.at[h, :, pl.ds(far, W)],
            send_sem=sx.at[h, int(up)],
            recv_sem=rx.at[h, int(up)],
            device_id={"row": lax.rem(me_r + (1 if up else rows - 1), rows)},
            device_id_type=MESH,
        )

    def ycopy(h, up):
        own, far = ((Y, 0) if up else (W, Y + W))
        return pltpu.make_async_remote_copy(
            src_ref=yb.at[h, :, :, pl.ds(own, W)],
            dst_ref=yb.at[h, :, :, pl.ds(far, W)],
            send_sem=sy.at[h, int(up)],
            recv_sem=ry.at[h, int(up)],
            device_id={"col": lax.rem(me_c + (1 if up else cols - 1), cols)},
            device_id_type=MESH,
        )

    PX = 8
    for h in range(halves):
        lanes = pl.ds(h * LANES, LANES)

        def zstep(i, unused):
            for f, ref in enumerate((gal, ran)):
                high, low = split(ref[pl.ds(i * PX, PX)].reshape(PX * Y, Z))
                th = thi[:, lanes]
                val = dot(high, th) + dot(high, tlo[:, lanes]) + dot(low, th)
                xb[h, f, pl.ds(W + i * PX, PX)] = val.reshape(PX, Y, LANES)
            return unused

        lax.fori_loop(0, X // PX, zstep, 0)

        @pl.when(me_r > 0)
        def _():
            xcopy(h, False).start()

        @pl.when(me_r < rows - 1)
        def _():
            xcopy(h, True).start()

        @pl.when(me_r == 0)
        def _():
            xb[h, :, 0:W] = jnp.zeros((2, W, Y, LANES), F32)

        @pl.when(me_r == rows - 1)
        def _():
            xb[h, :, X + W:] = jnp.zeros((2, W, Y, LANES), F32)

        @pl.when(me_c == 0)
        def _():
            yb[h, :, :, 0:W] = jnp.zeros((2, X, W, LANES), F32)

        @pl.when(me_c == cols - 1)
        def _():
            yb[h, :, :, Y + W:] = jnp.zeros((2, X, W, LANES), F32)

    def tstep(i, carry):
        m = cov[i].astype(F32)
        g = (m * gal[i]).reshape(Y // 8, 8, Z).sum(axis=0)
        r = (m * ran[i]).reshape(Y // 8, 8, Z).sum(axis=0)
        return carry[0] + g, carry[1] + r

    zero = jnp.zeros((8, Z), F32)
    tg, tr = lax.fori_loop(0, X, tstep, (zero, zero))
    for f, t in enumerate((tg, tr)):
        trow[me_r, f] = sum(t[:, k * LANES:(k + 1) * LANES] for k in range(Z // LANES))
    tcol[me_c] = add_up(gather_sum("row", rows, trow, s1, r1), trow, rows)
    tot = add_up(gather_sum("col", cols, tcol, s2, r2), tcol, cols)
    alpha = jnp.sum(tot[0], keepdims=True) / jnp.sum(tot[1], keepdims=True)

    acc[...] = jnp.zeros_like(acc)
    iota_hi = lax.broadcasted_iota(jnp.int32, (8, 2 * LANES), 0)
    iota_lo = lax.broadcasted_iota(jnp.int32, (16, 2 * LANES), 0)

    def finish(h):
        lanes = pl.ds(h * LANES, LANES)

        def cstep(i, unused):
            x4 = pl.ds(i * 4, 4)
            both = jnp.concatenate(
                [yb[h, f, x4].reshape(4 * (Y + 2 * W), LANES) for f in range(2)], axis=1
            )
            high, low = split(both)
            kh = kyhi[...]
            val = dot(kh, high) + dot(kylo[...], high) + dot(kh, low)
            m = cov[x4, :, lanes].astype(F32).reshape(4 * Y, LANES)
            nbar = alpha * val[:, LANES:]
            weight = 1.0 / (1.0 + 2.0 * nbar)
            c = m * weight * (val[:, :LANES] / nbar - 1.0)
            contrast[x4, :, lanes] = c.reshape(4, Y, LANES)
            return unused

        lax.fori_loop(0, X // 4, cstep, 0)

        def pstep(i, unused):
            lx, ly = i // (Y // 8), i % (Y // 8)
            ys = pl.ds(ly * 8, 8)

            def pair(ref):
                return jnp.concatenate([ref[2 * lx, ys, lanes], ref[2 * lx + 1, ys, lanes]], axis=1)

            c = pair(contrast)
            p = jnp.where(pair(cov) > 0, pair(pat), -1)
            phi, plo = p >> 4, p & 15
            vals = []
            power = c
            for q in range(3):
                high = power.astype(BF16).astype(F32)
                vals += [high, power - high]
                power = power * c
            lhs, rhs = [], []
            for s in range(8):
                def wide(v, n=8):
                    return jnp.broadcast_to(v[s:s + 1], (n, 2 * LANES))
                mask = wide(phi) == iota_hi
                parts = [jnp.where(mask, 1.0, 0.0)]
                parts += [jnp.where(mask, wide(v), 0.0) for v in vals]
                parts.append(jnp.zeros((8, 2 * LANES), F32))
                lhs.append(jnp.concatenate(parts, axis=0).astype(BF16))
                rhs.append(jnp.where(wide(plo, 16) == iota_lo, 1.0, 0.0).astype(BF16))
            acc[...] += lax.dot_general(
                jnp.concatenate(lhs, axis=1),
                jnp.concatenate(rhs, axis=1),
                (((1,), (1,)), ((), ())),
                preferred_element_type=F32,
            )
            return unused

        lax.fori_loop(0, X // 2 * (Y // 8), pstep, 0)

    for h in range(halves):
        @pl.when(me_r > 0)
        def _():
            xcopy(h, True).wait_recv()

        @pl.when(me_r < rows - 1)
        def _():
            xcopy(h, False).wait_recv()

        def xstep(t, unused):
            ys = pl.ds(t * 8, 8)
            both = jnp.concatenate(
                [xb[h, f, :, ys].reshape((X + 2 * W) * 8, LANES) for f in range(2)], axis=1
            )
            high, low = split(both)
            kh = kxhi[...]
            val = dot(kh, high) + dot(kxlo[...], high) + dot(kh, low)
            for f in range(2):
                yb[h, f, :, pl.ds(W + t * 8, 8)] = val[:, f * LANES:(f + 1) * LANES].reshape(X, 8, LANES)
            return unused

        lax.fori_loop(0, W // 8, xstep, 0)

        @pl.when(me_c > 0)
        def _():
            ycopy(h, False).start()

        lax.fori_loop(W // 8, Y // 8, xstep, 0)

        @pl.when(me_c < cols - 1)
        def _():
            ycopy(h, True).start()

        @pl.when(me_c > 0)
        def _():
            ycopy(h, True).wait_recv()

        @pl.when(me_c < cols - 1)
        def _():
            ycopy(h, False).wait_recv()

        finish(h)

    a = acc[...]
    terms = [a[0:8]] + [a[8 + 16 * q:16 + 16 * q] + a[16 + 16 * q:24 + 16 * q] for q in range(3)]
    spread = jnp.dot(
        jnp.concatenate(terms, axis=0), rep[...],
        precision=lax.Precision.HIGHEST, preferred_element_type=F32,
    )
    patch_hi = lax.broadcasted_iota(jnp.int32, (8, NPATCH), 1) // 16
    own = patch_hi == lax.broadcasted_iota(jnp.int32, (8, NPATCH), 0)
    for q in range(4):
        part = jnp.where(own, spread[8 * q:8 * q + 8], 0.0)
        srow[me_r, q:q + 1] = jnp.sum(part, axis=0, keepdims=True)
    srow[me_r, 4:8] = jnp.zeros((4, NPATCH), F32)
    scol[me_c] = add_up(gather_sum("row", rows, srow, s3, r3), srow, rows)
    whole = add_up(gather_sum("col", cols, scol, s4, r4), scol, cols)
    sums[...] = whole[0:4] * scale

    for h in range(halves):
        @pl.when(me_r > 0)
        def _():
            xcopy(h, False).wait_send()

        @pl.when(me_r < rows - 1)
        def _():
            xcopy(h, True).wait_send()

        @pl.when(me_c > 0)
        def _():
            ycopy(h, False).wait_send()

        @pl.when(me_c < cols - 1)
        def _():
            ycopy(h, True).wait_send()


def local(galaxy, randoms, coverage, patch):
    rows, cols = lax.axis_size("row"), lax.axis_size("col")
    X, Y, Z = galaxy.shape
    halves = Z // LANES
    W = RADIUS
    scale = NPATCH / (X * rows * Y * cols * Z)
    tz = split_np(band(Z, Z, 0).T)
    kx = split_np(np.kron(band(X, X + 2 * W, W), np.eye(8, dtype=np.float32)))
    ky = split_np(np.kron(np.eye(4, dtype=np.float32), band(Y, Y + 2 * W, W)))
    rep = (np.arange(NPATCH)[None, :] % 16 == np.arange(16)[:, None]).astype(np.float32)
    consts = [jnp.asarray(v) for v in (*tz, *kx, *ky, rep)]
    vmem = pl.BlockSpec(memory_space=pltpu.VMEM)
    dma = pltpu.SemaphoreType.DMA
    contrast, sums = pl.pallas_call(
        functools.partial(kernel, rows, cols, scale),
        out_shape=(
            jax.ShapeDtypeStruct((X, Y, Z), F32),
            jax.ShapeDtypeStruct((4, NPATCH), F32),
        ),
        in_specs=[vmem] * 11,
        out_specs=(vmem, vmem),
        scratch_shapes=[
            pltpu.VMEM((halves, 2, X + 2 * W, Y, LANES), F32),
            pltpu.VMEM((halves, 2, X, Y + 2 * W, LANES), F32),
            pltpu.VMEM((64, 16), F32),
            pltpu.VMEM((rows, 2, 8, LANES), F32),
            pltpu.VMEM((cols, 2, 8, LANES), F32),
            pltpu.VMEM((rows, 8, NPATCH), F32),
            pltpu.VMEM((cols, 8, NPATCH), F32),
            dma((halves, 2)), dma((halves, 2)), dma((halves, 2)), dma((halves, 2)),
            dma((rows - 1,)), dma((rows - 1,)), dma((cols - 1,)), dma((cols - 1,)),
            dma((rows - 1,)), dma((rows - 1,)), dma((cols - 1,)), dma((cols - 1,)),
        ],
        compiler_params=pltpu.CompilerParams(
            collective_id=0, has_side_effects=True, vmem_limit_bytes=40 * 1024 * 1024
        ),
    )(galaxy, randoms, coverage, patch, *consts)
    return contrast, sums


def solution(mesh):
    spec = P("row", "col", None)
    return jax.shard_map(
        local, mesh=mesh, in_specs=(spec,) * 4, out_specs=(spec, P()), check_vma=False
    )
```

time: 387 us -> 128 us (0.33)
  other arithmetic: 153 us -> 0 us
  Pallas kernels: 0 us -> 114 us
  blocking collectives: 88 us -> 0 us
  matrix products: 64.8 us -> 0 us
  waiting for transfers between devices: 45.5 us -> 0 us
  starting transfers between devices: 10.1 us -> 0 us
  local copies, waits for them, and re-layouts: 20.9 us -> 12.5 us
    add x3 -> x0, other arithmetic: 130 us -> none  [valid_taps(): total = total + taps[j] * lax.slice_in_dim(padded, j, j + count, axis=axis)]
    pallas_call x0 -> x1, Pallas kernels: none -> 114 us  [local(): pl.pallas_call(functools.partial(kernel, rows, cols, scale), out_shape=(j...]
    psum x2 -> x0, blocking collectives: 88 us -> none  [the longest x1 46.6 us: local(): lax.psum((jnp.sum(cover * galaxy), jnp.sum(cover * randoms)), ('row', 'co...]
    dot_general x8 -> x0, matrix products: 64.8 us -> none  [accumulate(): lax.dot_general(powers, onehot, (((1,), (1,)), ((), ())), precision=lax.P...]
    ppermute x4 -> x0, waiting for transfers between devices: 45.5 us -> none  [the longest x2 24.4 us: extended_2(): after = lax.ppermute(first, axis, down)]
    mul x10 -> x0, other arithmetic: 13 us -> none  [the longest x8 12 us: accumulate(): mvals * cvals * cvals * cvals]
    unnamed x12 -> x24, local copies, waits for them, and re-layouts: 1.21 us -> 12.5 us
    dynamic_slice x8 -> x0, local copies, waits for them, and re-layouts: 10.6 us -> none  [local(): lax.scan(accumulate, jnp.zeros((4, NPATCH), jnp.float32), (flat_c, flat_m...]
  transfers between devices with their start and end apart: 4 -> 0, of which waited for: 2 -> 0; matrix products, arithmetic and copies ran while one was open for 2% -> 0% of each run, Pallas kernels for 0% -> 0%
where the time goes in v1:
time: 128 us
  Pallas kernels  114 us (89%)
  local copies, waits for them, and re-layouts  12.5 us (10%)
    pallas_call x1, Pallas kernels, local(): pl.pallas_call(functools.partial(kernel, rows, cols, scale), out_shape=(j...  114 us
    unnamed x24, local copies, waits for them, and re-layouts  12.5 us

profile of v1, /device:TPU:0, one launch (start us, length us, event | category | flops | bytes accessed | tf_op | source)
XLA Modules:
  0.0 127.6 jit_solution(14970704987107479733)
XLA Ops:
  0.6 0.0 copy-start.10
  0.6 0.7 copy-done.10
  1.3 0.0 copy-start
  1.3 1.2 copy-done
  2.6 0.0 copy-start.1
  2.6 1.2 copy-done.1
  3.8 0.0 copy-start.2
  3.8 1.2 copy-done.2
  5.0 0.0 copy-start.3
  5.0 1.2 copy-done.3
  6.2 0.0 copy-start.4
  6.2 0.9 copy-done.4
  7.2 0.0 copy-start.5
  7.2 0.9 copy-done.5
  8.1 0.0 copy-start.6
  8.1 0.9 copy-done.6
  9.0 0.0 copy-start.7
  9.0 0.9 copy-done.7
  9.9 0.0 copy-start.8
  9.9 0.8 copy-done.8
  10.8 0.0 copy-start.9
  10.8 0.8 copy-done.9
  11.6 114.4 %shard_map.122 = (f32[32,32,256]{2,1,0:T(8,128)S(1)}, f32[4,128]{1,0:T(4,128)S(1)}) custom-call(f32[32,32,256]{2,1,0:T(8,128)S(1)} %copy-done, f32[32,32,256]{2,1,0:T(8,128)S(1)} %copy-done.1, s32[32,32,256]{2,1,0:T(8,128)S(1)} %copy-done.2, s32[32,32,256]{2,1,0:T(8,128)S(1)} %copy-done.3, bf16[256,256]{1,0:T(8,128)(2,1)S(1)} %copy-done.7, ...), custom_call_target="tpu_custom_call" | custom-call | tf_op jit(solution)/shard_map/pallas_call | solution.py:324
  126.1 1.0 copy.15
  127.1 0.6 copy.16
Async XLA Ops:
  0.6 0.7 copy-start.10
  1.3 1.2 copy-start
  2.6 1.2 copy-start.1
  3.8 1.2 copy-start.2
  5.0 1.2 copy-start.3
  6.2 0.9 copy-start.4
  7.2 0.9 copy-start.5
  8.1 0.9 copy-start.6
  9.0 0.9 copy-start.7
  9.9 0.8 copy-start.8
  10.8 0.8 copy-start.9

commit v2 on v1

--- a/solution.py
+++ b/solution.py
@@ -79,23 +79,43 @@
 
 def kernel(
     rows, cols, scale,
-    gal, ran, cov, pat, thi, tlo, kxhi, kxlo, kyhi, kylo, rep,
-    contrast, sums,
-    xb, yb, acc, trow, tcol, srow, scol,
-    sx, rx, sy, ry, s1, r1, s2, r2, s3, r3, s4, r4,
+    *refs,
 ):
+    hbm, (contrast, sums), vmem = refs[:11], refs[11:13], refs[13:24]
+    (
+        xb, yb, acc, trow, tcol, srow, scol, sin,
+        sx, rx, sy, ry, s1, r1, s2, r2, s3, r3, s4, r4,
+    ) = refs[24:]
+    gal, ran, cov, pat, thi, tlo, kxhi, kxlo, kyhi, kylo, rep = vmem
     X, Y, Z = gal.shape
     halves = Z // LANES
     W = RADIUS
     me_r = lax.axis_index("row")
     me_c = lax.axis_index("col")
 
+    PX = 8
+    slabs = X // PX
+    def fetch(k, slab=None):
+        at = slice(None) if slab is None else pl.ds(slab * PX, PX)
+        return pltpu.make_async_copy(
+            hbm[k].at[at], vmem[k].at[at], sin.at[k, 0 if slab is None else slab]
+        )
+
+    fetch(4).start()
+    fetch(5).start()
+    for i in range(slabs):
+        fetch(0, i).start()
+        fetch(1, i).start()
+    for k in (6, 7, 2, 8, 9, 3, 10):
+        fetch(k).start()
+
     barrier = pltpu.get_barrier_semaphore()
     for k in range(1, rows):
         pl.semaphore_signal(barrier, inc=1, device_id={"row": lax.rem(me_r + k, rows)}, device_id_type=MESH)
     for k in range(1, cols):
         pl.semaphore_signal(barrier, inc=1, device_id={"col": lax.rem(me_c + k, cols)}, device_id_type=MESH)
-    pl.semaphore_wait(barrier, rows + cols - 2)
+    fetch(4).wait()
+    fetch(5).wait()
 
     def xcopy(h, up):
         own, far = ((X, 0) if up else (W, X + W))
@@ -119,7 +139,24 @@
             device_id_type=MESH,
         )
 
-    PX = 8
+    def xstart(h):
+        @pl.when(me_r > 0)
+        def _():
+            xcopy(h, False).start()
+
+        @pl.when(me_r < rows - 1)
+        def _():
+            xcopy(h, True).start()
+
+    def xsent(h):
+        @pl.when(me_r > 0)
+        def _():
+            xcopy(h, False).wait_send()
+
+        @pl.when(me_r < rows - 1)
+        def _():
+            xcopy(h, True).wait_send()
+
     for h in range(halves):
         lanes = pl.ds(h * LANES, LANES)
 
@@ -131,15 +168,14 @@
                 xb[h, f, pl.ds(W + i * PX, PX)] = val.reshape(PX, Y, LANES)
             return unused
 
-        lax.fori_loop(0, X // PX, zstep, 0)
-
-        @pl.when(me_r > 0)
-        def _():
-            xcopy(h, False).start()
-
-        @pl.when(me_r < rows - 1)
-        def _():
-            xcopy(h, True).start()
+        for i in range(slabs):
+            if h == 0:
+                fetch(0, i).wait()
+                fetch(1, i).wait()
+            zstep(i, 0)
+        if h == 0:
+            pl.semaphore_wait(barrier, rows + cols - 2)
+            xstart(h)
 
         @pl.when(me_r == 0)
         def _():
@@ -156,6 +192,9 @@
         @pl.when(me_c == cols - 1)
         def _():
             yb[h, :, :, Y + W:] = jnp.zeros((2, X, W, LANES), F32)
+
+    for k in (2, 3, 6, 7, 8, 9, 10):
+        fetch(k).wait()
 
     def tstep(i, carry):
         m = cov[i].astype(F32)
@@ -240,6 +279,10 @@
         def _():
             xcopy(h, False).wait_recv()
 
+        xsent(h)
+        if h + 1 < halves:
+            xstart(h + 1)
+
         def xstep(t, unused):
             ys = pl.ds(t * 8, 8)
             both = jnp.concatenate(
@@ -291,14 +334,6 @@
     sums[...] = whole[0:4] * scale
 
     for h in range(halves):
-        @pl.when(me_r > 0)
-        def _():
-            xcopy(h, False).wait_send()
-
-        @pl.when(me_r < rows - 1)
-        def _():
-            xcopy(h, True).wait_send()
-
         @pl.when(me_c > 0)
         def _():
             ycopy(h, False).wait_send()
@@ -319,6 +354,7 @@
     ky = split_np(np.kron(np.eye(4, dtype=np.float32), band(Y, Y + 2 * W, W)))
     rep = (np.arange(NPATCH)[None, :] % 16 == np.arange(16)[:, None]).astype(np.float32)
     consts = [jnp.asarray(v) for v in (*tz, *kx, *ky, rep)]
+    args = (galaxy, randoms, coverage, patch, *consts)
     vmem = pl.BlockSpec(memory_space=pltpu.VMEM)
     dma = pltpu.SemaphoreType.DMA
     contrast, sums = pl.pallas_call(
@@ -327,9 +363,9 @@
             jax.ShapeDtypeStruct((X, Y, Z), F32),
             jax.ShapeDtypeStruct((4, NPATCH), F32),
         ),
-        in_specs=[vmem] * 11,
+        in_specs=[pl.BlockSpec(memory_space=pl.ANY)] * 11,
         out_specs=(vmem, vmem),
-        scratch_shapes=[
+        scratch_shapes=[pltpu.VMEM(v.shape, v.dtype) for v in args] + [
             pltpu.VMEM((halves, 2, X + 2 * W, Y, LANES), F32),
             pltpu.VMEM((halves, 2, X, Y + 2 * W, LANES), F32),
             pltpu.VMEM((64, 16), F32),
@@ -337,14 +373,15 @@
             pltpu.VMEM((cols, 2, 8, LANES), F32),
             pltpu.VMEM((rows, 8, NPATCH), F32),
             pltpu.VMEM((cols, 8, NPATCH), F32),
+            dma((11, X // 8)),
             dma((halves, 2)), dma((halves, 2)), dma((halves, 2)), dma((halves, 2)),
             dma((rows - 1,)), dma((rows - 1,)), dma((cols - 1,)), dma((cols - 1,)),
             dma((rows - 1,)), dma((rows - 1,)), dma((cols - 1,)), dma((cols - 1,)),
         ],
         compiler_params=pltpu.CompilerParams(
-            collective_id=0, has_side_effects=True, vmem_limit_bytes=40 * 1024 * 1024
+            collective_id=0, has_side_effects=True, vmem_limit_bytes=60 * 1024 * 1024
         ),
-    )(galaxy, randoms, coverage, patch, *consts)
+    )(*args)
     return contrast, sums
 
 

time: 128 us -> 96.1 us (0.75)
  Pallas kernels: 114 us -> 92.4 us
  local copies, waits for them, and re-layouts: 12.5 us -> 2.89 us
    pallas_call x1, Pallas kernels: 114 us -> 92.4 us  [local(): pl.pallas_call(functools.partial(kernel, rows, cols, scale), out_shape=(j...]
    unnamed x24 -> x4, local copies, waits for them, and re-layouts: 12.5 us -> 2.89 us
where the time goes in v2:
time: 96.1 us; the launch traced here: 95.9 us
  Pallas kernels  92.4 us (96%)
  local copies, waits for them, and re-layouts  2.89 us (3%)
    pallas_call x1, Pallas kernels, local(): pl.pallas_call(functools.partial(kernel, rows, cols, scale), out_shape=(j...  92.4 us
    unnamed x4, local copies, waits for them, and re-layouts  2.89 us

profile of v2, /device:TPU:0, one launch (start us, length us, event | category | flops | bytes accessed | tf_op | source)
XLA Modules:
  0.0 95.9 jit_solution(14090884841463357218)
XLA Ops:
  0.6 92.4 %shard_map.122 = (f32[32,32,256]{2,1,0:T(8,128)}, f32[4,128]{1,0:T(4,128)}) custom-call(f32[32,32,256]{2,1,0:T(8,128)} %refs_0_.1, f32[32,32,256]{2,1,0:T(8,128)} %refs_1_.1, s32[32,32,256]{2,1,0:T(8,128)} %refs_2_.1, s32[32,32,256]{2,1,0:T(8,128)} %refs_3_.1, bf16[256,256]{1,0:T(8,128)(2,1)} %constant.14.clone.refs_4_, ...), custom_call_target="tpu_custom_call" | custom-call | tf_op jit(solution)/shard_map/pallas_call | solution.py:360
  93.0 0.0 copy-start
  93.1 2.3 %copy.15 = f32[32,32,256]{2,1,0:T(8,128)} copy(f32[32,32,256]{2,1,0:T(8,128)} %get-tuple-element.4) | data formatting | bytes 2097152
  95.4 0.0 copy-done
  95.4 0.6 copy.16
Async XLA Ops:
  93.0 2.3 %copy-start = (f32[4,128]{1,0:T(4,128)S(1)}, f32[4,128]{1,0:T(4,128)}, u32[]{:S(2)}) copy-start(f32[4,128]{1,0:T(4,128)} %get-tuple-element.5) | copy-start | bytes 6148

commit v3 on v2

--- a/solution.py
+++ b/solution.py
@@ -83,8 +83,8 @@
 ):
     hbm, (contrast, sums), vmem = refs[:11], refs[11:13], refs[13:24]
     (
-        xb, yb, acc, trow, tcol, srow, scol, sin,
-        sx, rx, sy, ry, s1, r1, s2, r2, s3, r3, s4, r4,
+        xb, yb, acc, trow, tcol, srow, scol, rb, oh, rh, sin,
+        sx, rx, sy, ry, srel, rrel, s1, r1, s2, r2, s3, r3, s4, r4,
     ) = refs[24:]
     gal, ran, cov, pat, thi, tlo, kxhi, kxlo, kyhi, kylo, rep = vmem
     X, Y, Z = gal.shape
@@ -117,16 +117,71 @@
     fetch(4).wait()
     fetch(5).wait()
 
-    def xcopy(h, up):
-        own, far = ((X, 0) if up else (W, X + W))
+    relayed = rows == 4
+    YP = Y // 2
+
+    def xsrc(h, up, part):
+        return xb.at[h, :, pl.ds(X if up else W, W), pl.ds(part * YP, YP)]
+
+    def xdst(h, up, part):
+        return xb.at[h, :, pl.ds(0 if up else X + W, W), pl.ds(part * YP, YP)]
+
+    def xsend(src, dst, ssem, rsem, hop):
         return pltpu.make_async_remote_copy(
-            src_ref=xb.at[h, :, pl.ds(own, W)],
-            dst_ref=xb.at[h, :, pl.ds(far, W)],
-            send_sem=sx.at[h, int(up)],
-            recv_sem=rx.at[h, int(up)],
-            device_id={"row": lax.rem(me_r + (1 if up else rows - 1), rows)},
-            device_id_type=MESH,
+            src_ref=src, dst_ref=dst, send_sem=ssem, recv_sem=rsem,
+            device_id={"row": lax.rem(me_r + (hop + rows), rows)}, device_id_type=MESH,
         )
+
+    def xcopy(h, up, part):
+        u = int(up)
+        return xsend(xsrc(h, up, part), xdst(h, up, part), sx.at[h, u, part], rx.at[h, u, part], 1 if up else -1)
+
+    def xfirst(h, up):
+        return xsend(xsrc(h, up, 1), rb.at[h], sx.at[h, int(up), 1], rrel.at[h], 2 if up else -2)
+
+    def xsecond(h, up):
+        return xsend(rb.at[h], xdst(h, up, 1), srel.at[h], rx.at[h, int(up), 1], -1 if up else 1)
+
+    def xeach(h, act):
+        for part in (1, 0):
+            for up in (False, True):
+                has = me_r < rows - 1 if up else me_r > 0
+                if relayed and part == 1:
+                    turn = me_r == (1 if up else 2)
+
+                    @pl.when(turn)
+                    def _():
+                        act(xfirst(h, up))
+
+                    has = jnp.logical_and(has, jnp.logical_not(turn))
+
+                @pl.when(has)
+                def _():
+                    act(xcopy(h, up, part))
+
+    def relay(h, act):
+        if relayed:
+            for up in (False, True):
+                @pl.when(me_r == (3 if up else 0))
+                def _():
+                    act(xsecond(h, up))
+
+    def relay_on(h):
+        if relayed:
+            for up in (False, True):
+                @pl.when(me_r == (3 if up else 0))
+                def _():
+                    xfirst(h, up).wait_recv()
+                    xsecond(h, up).start()
+
+    def xarrived(h, part):
+        @pl.when(me_r > 0)
+        def _():
+            xcopy(h, True, part).wait_recv()
+
+        @pl.when(me_r < rows - 1)
+        def _():
+            xcopy(h, False, part).wait_recv()
 
     def ycopy(h, up):
         own, far = ((Y, 0) if up else (W, Y + W))
@@ -140,22 +195,10 @@
         )
 
     def xstart(h):
-        @pl.when(me_r > 0)
-        def _():
-            xcopy(h, False).start()
-
-        @pl.when(me_r < rows - 1)
-        def _():
-            xcopy(h, True).start()
+        xeach(h, lambda copy: copy.start())
 
     def xsent(h):
-        @pl.when(me_r > 0)
-        def _():
-            xcopy(h, False).wait_send()
-
-        @pl.when(me_r < rows - 1)
-        def _():
-            xcopy(h, True).wait_send()
+        xeach(h, lambda copy: copy.wait_send())
 
     for h in range(halves):
         lanes = pl.ds(h * LANES, LANES)
@@ -206,15 +249,33 @@
     tg, tr = lax.fori_loop(0, X, tstep, (zero, zero))
     for f, t in enumerate((tg, tr)):
         trow[me_r, f] = sum(t[:, k * LANES:(k + 1) * LANES] for k in range(Z // LANES))
-    tcol[me_c] = add_up(gather_sum("row", rows, trow, s1, r1), trow, rows)
-    tot = add_up(gather_sum("col", cols, tcol, s2, r2), tcol, cols)
-    alpha = jnp.sum(tot[0], keepdims=True) / jnp.sum(tot[1], keepdims=True)
+    row_totals = gather_sum("row", rows, trow, s1, r1)
 
     acc[...] = jnp.zeros_like(acc)
-    iota_hi = lax.broadcasted_iota(jnp.int32, (8, 2 * LANES), 0)
-    iota_lo = lax.broadcasted_iota(jnp.int32, (16, 2 * LANES), 0)
-
-    def finish(h):
+    iota = lax.broadcasted_iota(jnp.int32, (8, 2 * LANES), 0)
+
+    def pair(ref, h, i):
+        lx, ys, lanes = i // (Y // 8), pl.ds(i % (Y // 8) * 8, 8), pl.ds(h * LANES, LANES)
+        return jnp.concatenate([ref[2 * lx, ys, lanes], ref[2 * lx + 1, ys, lanes]], axis=1)
+
+    def wide(v, s):
+        return jnp.broadcast_to(v[s:s + 1], (8, 2 * LANES))
+
+    def onehots(h):
+        def step(i, unused):
+            p = jnp.where(pair(cov, h, i) > 0, pair(pat, h, i), -1)
+            phi, plo = p >> 4, p & 15
+            for s in range(8):
+                at = pl.ds(s * 2 * LANES, 2 * LANES)
+                one = jnp.where(wide(phi, s) == iota, 1.0, 0.0)
+                oh[h, i, :, at] = jnp.concatenate([one, one], axis=0).astype(BF16)
+                lows = [jnp.where(wide(plo, s) == iota + k, 1.0, 0.0) for k in (0, 8)]
+                rh[h, i, :, at] = jnp.concatenate(lows, axis=0).astype(BF16)
+            return unused
+
+        lax.fori_loop(0, X // 2 * (Y // 8), step, 0)
+
+    def finish(h, alpha):
         lanes = pl.ds(h * LANES, LANES)
 
         def cstep(i, unused):
@@ -235,35 +296,19 @@
         lax.fori_loop(0, X // 4, cstep, 0)
 
         def pstep(i, unused):
-            lx, ly = i // (Y // 8), i % (Y // 8)
-            ys = pl.ds(ly * 8, 8)
-
-            def pair(ref):
-                return jnp.concatenate([ref[2 * lx, ys, lanes], ref[2 * lx + 1, ys, lanes]], axis=1)
-
-            c = pair(contrast)
-            p = jnp.where(pair(cov) > 0, pair(pat), -1)
-            phi, plo = p >> 4, p & 15
-            vals = []
+            c = pair(contrast, h, i)
+            terms = [oh[h, i]]
             power = c
             for q in range(3):
-                high = power.astype(BF16).astype(F32)
-                vals += [high, power - high]
+                high, low = split(power)
+                high, low = high.astype(F32), low.astype(F32)
+                terms.append(jnp.concatenate([
+                    jnp.concatenate([wide(high, s), wide(low, s)], axis=0).astype(BF16)
+                    for s in range(8)
+                ], axis=1) * oh[h, i])
                 power = power * c
-            lhs, rhs = [], []
-            for s in range(8):
-                def wide(v, n=8):
-                    return jnp.broadcast_to(v[s:s + 1], (n, 2 * LANES))
-                mask = wide(phi) == iota_hi
-                parts = [jnp.where(mask, 1.0, 0.0)]
-                parts += [jnp.where(mask, wide(v), 0.0) for v in vals]
-                parts.append(jnp.zeros((8, 2 * LANES), F32))
-                lhs.append(jnp.concatenate(parts, axis=0).astype(BF16))
-                rhs.append(jnp.where(wide(plo, 16) == iota_lo, 1.0, 0.0).astype(BF16))
             acc[...] += lax.dot_general(
-                jnp.concatenate(lhs, axis=1),
-                jnp.concatenate(rhs, axis=1),
-                (((1,), (1,)), ((), ())),
+                rh[h, i], jnp.concatenate(terms, axis=0), (((1,), (1,)), ((), ())),
                 preferred_element_type=F32,
             )
             return unused
@@ -271,18 +316,6 @@
         lax.fori_loop(0, X // 2 * (Y // 8), pstep, 0)
 
     for h in range(halves):
-        @pl.when(me_r > 0)
-        def _():
-            xcopy(h, True).wait_recv()
-
-        @pl.when(me_r < rows - 1)
-        def _():
-            xcopy(h, False).wait_recv()
-
-        xsent(h)
-        if h + 1 < halves:
-            xstart(h + 1)
-
         def xstep(t, unused):
             ys = pl.ds(t * 8, 8)
             both = jnp.concatenate(
@@ -295,18 +328,32 @@
                 yb[h, f, :, pl.ds(W + t * 8, 8)] = val[:, f * LANES:(f + 1) * LANES].reshape(X, 8, LANES)
             return unused
 
+        if h == 0:
+            relay_on(0)
+            onehots(0)
+        xarrived(h, 0)
+        if h == 0:
+            tcol[me_c] = add_up(row_totals, trow, rows)
+            col_totals = gather_sum("col", cols, tcol, s2, r2)
         lax.fori_loop(0, W // 8, xstep, 0)
 
         @pl.when(me_c > 0)
         def _():
             ycopy(h, False).start()
 
+        xarrived(h, 1)
+        xsent(h)
+        if h + 1 < halves:
+            xstart(h + 1)
         lax.fori_loop(W // 8, Y // 8, xstep, 0)
 
         @pl.when(me_c < cols - 1)
         def _():
             ycopy(h, True).start()
 
+        if h > 0:
+            onehots(h)
+
         @pl.when(me_c > 0)
         def _():
             ycopy(h, True).wait_recv()
@@ -315,10 +362,15 @@
         def _():
             ycopy(h, False).wait_recv()
 
-        finish(h)
-
-    a = acc[...]
-    terms = [a[0:8]] + [a[8 + 16 * q:16 + 16 * q] + a[16 + 16 * q:24 + 16 * q] for q in range(3)]
+        if h + 1 < halves:
+            relay_on(h + 1)
+        if h == 0:
+            tot = add_up(col_totals, tcol, cols)
+            alpha = jnp.sum(tot[0], keepdims=True) / jnp.sum(tot[1], keepdims=True)
+        finish(h, alpha)
+
+    a = acc[...].T
+    terms = [a[0:8]] + [a[16 * q:16 * q + 8] + a[16 * q + 8:16 * q + 16] for q in range(1, 4)]
     spread = jnp.dot(
         jnp.concatenate(terms, axis=0), rep[...],
         precision=lax.Precision.HIGHEST, preferred_element_type=F32,
@@ -334,6 +386,8 @@
     sums[...] = whole[0:4] * scale
 
     for h in range(halves):
+        relay(h, lambda copy: copy.wait_send())
+
         @pl.when(me_c > 0)
         def _():
             ycopy(h, False).wait_send()
@@ -368,13 +422,17 @@
         scratch_shapes=[pltpu.VMEM(v.shape, v.dtype) for v in args] + [
             pltpu.VMEM((halves, 2, X + 2 * W, Y, LANES), F32),
             pltpu.VMEM((halves, 2, X, Y + 2 * W, LANES), F32),
-            pltpu.VMEM((64, 16), F32),
+            pltpu.VMEM((16, 64), F32),
             pltpu.VMEM((rows, 2, 8, LANES), F32),
             pltpu.VMEM((cols, 2, 8, LANES), F32),
             pltpu.VMEM((rows, 8, NPATCH), F32),
             pltpu.VMEM((cols, 8, NPATCH), F32),
+            pltpu.VMEM((halves, 2, W, Y // 2, LANES), F32),
+            pltpu.VMEM((halves, X // 2 * (Y // 8), 16, 16 * LANES), BF16),
+            pltpu.VMEM((halves, X // 2 * (Y // 8), 16, 16 * LANES), BF16),
             dma((11, X // 8)),
-            dma((halves, 2)), dma((halves, 2)), dma((halves, 2)), dma((halves, 2)),
+            dma((halves, 2, 2)), dma((halves, 2, 2)), dma((halves, 2)), dma((halves, 2)),
+            dma((halves,)), dma((halves,)),
             dma((rows - 1,)), dma((rows - 1,)), dma((cols - 1,)), dma((cols - 1,)),
             dma((rows - 1,)), dma((rows - 1,)), dma((cols - 1,)), dma((cols - 1,)),
         ],

time: 96.1 us -> 85.1 us (0.89)
  Pallas kernels: 92.4 us -> 81.4 us
    pallas_call x1, Pallas kernels: 92.4 us -> 81.4 us  [local(): pl.pallas_call(functools.partial(kernel, rows, cols, scale), out_shape=(j...]
where the time goes in v3:
time: 85.1 us; the launch traced here: 85 us
  Pallas kernels  81.4 us (96%)
  local copies, waits for them, and re-layouts  2.89 us (3%)
    pallas_call x1, Pallas kernels, local(): pl.pallas_call(functools.partial(kernel, rows, cols, scale), out_shape=(j...  81.4 us
    unnamed x4, local copies, waits for them, and re-layouts  2.89 us

profile of v3, /device:TPU:0, one launch (start us, length us, event | category | flops | bytes accessed | tf_op | source)
XLA Modules:
  0.0 85.0 jit_solution(9438343205927202365)
XLA Ops:
  0.6 81.4 %shard_map.122 = (f32[32,32,256]{2,1,0:T(8,128)}, f32[4,128]{1,0:T(4,128)}) custom-call(f32[32,32,256]{2,1,0:T(8,128)} %refs_0_.1, f32[32,32,256]{2,1,0:T(8,128)} %refs_1_.1, s32[32,32,256]{2,1,0:T(8,128)} %refs_2_.1, s32[32,32,256]{2,1,0:T(8,128)} %refs_3_.1, bf16[256,256]{1,0:T(8,128)(2,1)} %constant.14.clone.refs_4_, ...), custom_call_target="tpu_custom_call" | custom-call | tf_op jit(solution)/shard_map/pallas_call | solution.py:414
  82.1 0.0 copy-start
  82.1 2.3 %copy.15 = f32[32,32,256]{2,1,0:T(8,128)} copy(f32[32,32,256]{2,1,0:T(8,128)} %get-tuple-element.4) | data formatting | bytes 2097152
  84.4 0.0 copy-done
  84.4 0.6 copy.16
Async XLA Ops:
  82.1 2.3 %copy-start = (f32[4,128]{1,0:T(4,128)S(1)}, f32[4,128]{1,0:T(4,128)}, u32[]{:S(2)}) copy-start(f32[4,128]{1,0:T(4,128)} %get-tuple-element.5) | copy-start | bytes 6148

commit v4 on v3

--- a/solution.py
+++ b/solution.py
@@ -273,7 +273,7 @@
                 rh[h, i, :, at] = jnp.concatenate(lows, axis=0).astype(BF16)
             return unused
 
-        lax.fori_loop(0, X // 2 * (Y // 8), step, 0)
+        lax.fori_loop(0, X // 2 * (Y // 8), step, 0, unroll=2)
 
     def finish(h, alpha):
         lanes = pl.ds(h * LANES, LANES)
@@ -293,7 +293,7 @@
             contrast[x4, :, lanes] = c.reshape(4, Y, LANES)
             return unused
 
-        lax.fori_loop(0, X // 4, cstep, 0)
+        lax.fori_loop(0, X // 4, cstep, 0, unroll=2)
 
         def pstep(i, unused):
             c = pair(contrast, h, i)
@@ -313,7 +313,7 @@
             )
             return unused
 
-        lax.fori_loop(0, X // 2 * (Y // 8), pstep, 0)
+        lax.fori_loop(0, X // 2 * (Y // 8), pstep, 0, unroll=4)
 
     for h in range(halves):
         def xstep(t, unused):

time: 85.1 us -> 72 us (0.85)
  Pallas kernels: 81.4 us -> 68.3 us
    pallas_call x1, Pallas kernels: 81.4 us -> 68.3 us  [local(): pl.pallas_call(functools.partial(kernel, rows, cols, scale), out_shape=(j...]
where the time goes in v4:
time: 72 us; the launch traced here: 71.8 us
  Pallas kernels  68.3 us (95%)
  local copies, waits for them, and re-layouts  2.89 us (4%)
    pallas_call x1, Pallas kernels, local(): pl.pallas_call(functools.partial(kernel, rows, cols, scale), out_shape=(j...  68.3 us
    unnamed x4, local copies, waits for them, and re-layouts  2.89 us

profile of v4, /device:TPU:0, one launch (start us, length us, event | category | flops | bytes accessed | tf_op | source)
XLA Modules:
  0.0 71.8 jit_solution(10063357859331588299)
XLA Ops:
  0.6 68.3 %shard_map.122 = (f32[32,32,256]{2,1,0:T(8,128)}, f32[4,128]{1,0:T(4,128)}) custom-call(f32[32,32,256]{2,1,0:T(8,128)} %refs_0_.1, f32[32,32,256]{2,1,0:T(8,128)} %refs_1_.1, s32[32,32,256]{2,1,0:T(8,128)} %refs_2_.1, s32[32,32,256]{2,1,0:T(8,128)} %refs_3_.1, bf16[256,256]{1,0:T(8,128)(2,1)} %constant.14.clone.refs_4_, ...), custom_call_target="tpu_custom_call" | custom-call | tf_op jit(solution)/shard_map/pallas_call | solution.py:414
  68.9 0.0 copy-start
  68.9 2.3 %copy.15 = f32[32,32,256]{2,1,0:T(8,128)} copy(f32[32,32,256]{2,1,0:T(8,128)} %get-tuple-element.4) | data formatting | bytes 2097152
  71.2 0.0 copy-done
  71.2 0.6 copy.16
Async XLA Ops:
  68.9 2.3 %copy-start = (f32[4,128]{1,0:T(4,128)S(1)}, f32[4,128]{1,0:T(4,128)}, u32[]{:S(2)}) copy-start(f32[4,128]{1,0:T(4,128)} %get-tuple-element.5) | copy-start | bytes 6148
